TPU v7x, 768 devices: a whole 4x8x12 slice. The times are simulated.
768 devices in a mesh: dom: 24 (over z, core), grp: 32 (over x, y).
Axes of the slice: x: 4, y: 8, z: 12, core: 2. Of those that a mesh axis runs over, the one named last changes fastest.
Arguments:
- features: bfloat16 [786432, 256], P(('dom', 'grp')), may hold values from -6 to 6
- w_self: bfloat16 [256, 256], replicated, may hold values from -0.375 to 0.375
- w_neigh: bfloat16 [256, 256], replicated, may hold values from -0.375 to 0.375
- degree: float32 [786432], P(('dom', 'grp')), may hold values from 1 to 8
- send_rows: int32 [18432, 16], P(('dom', 'grp')), may hold values from 0 to 1023, as said below
- inner_tiles: bfloat16 [19968, 128, 128], P(('dom', 'grp')), may hold values from 0.0019989014 to 0.059814453
- inner_blocks: int32 [19968, 2], P(('dom', 'grp')), may hold values from 0 to 10, as said below
- outer_tiles: bfloat16 [11520, 128, 128], P(('dom', 'grp')), may hold values from 0.0019989014 to 0.059814453
- outer_blocks: int32 [11520, 2], P(('dom', 'grp')), may hold values from 0 to 10, as said below
- tile_counts: int32 [768, 2], P(('dom', 'grp')), may hold values from 1 to 26, as said below
- d_out: bfloat16 [786432, 256], P(('dom', 'grp')), may hold values from -6 to 6
- d_mirror: bfloat16 [294912, 256], P(('dom', 'grp')), may hold values from -6 to 6
Outputs:
- out: bfloat16 [786432, 256], P(('dom', 'grp'))
- mirror_out: bfloat16 [294912, 256], P(('dom', 'grp'))
- grad_h: bfloat16 [786432, 256], P(('dom', 'grp'))
- grad_wself: float32 [256, 256], replicated
- grad_wneigh: float32 [256, 256], replicated
Inputs may be any that keep to these rules, and one draw needn't show every extreme that they name: `send_rows`: the 16 rows that one device lists for one peer are distinct. `inner_blocks`: each row is (destination block, source block) of slot blocks of 128 rows; the pairs of one device are distinct; sources are master blocks. `outer_blocks`: each row is (destination block, source block); the pairs of one device are distinct; sources are mirror blocks, from 8 on; destinations any block. `tile_counts`: column 0 counts the live leading inner tiles of a device, at most 26; column 1 the live outer tiles, at most 15; in every draw some device has 26 live inner tiles and some device 15 live outer tiles.
All inputs are finite; a program needn't handle non-finite values.
Results may differ from a plain program's by a relative error of at most 0.0057.
Values may be sent and summed in bfloat16 or wider, within the bound.
No kernel may reach another device: no remote copies, remote signals or barrier semaphores. Data moves between devices by JAX's collectives and lax.ppermute only.
A program may use at most 64 MiB of HBM per device.

v0:
```python
import functools

import jax
import jax.numpy as jnp
from jax import lax
from jax.experimental import pallas as pl
from jax.experimental.pallas import tpu as pltpu
from jax.sharding import PartitionSpec as P

BLOCK = 128
TILE = 16
BF16 = jnp.bfloat16
F32 = jnp.float32
NN = (((1,), (0,)), ((), ()))
TN = (((0,), (0,)), ((), ()))
NT = (((1,), (1,)), ((), ()))
ROOM = 62_500_000
LITTLE = 8_000_000


def dot(a, b, dims=NN):
    return lax.dot_general(a, b, dims, preferred_element_type=F32)


def one_hot(mask):
    return jnp.where(mask, 1.0, 0.0).astype(BF16)


def iota(shape, dim):
    return lax.broadcasted_iota(jnp.int32, shape, dim)


def narrow(value):
    return value.astype(F32).astype(BF16)


def index_column(send):
    each, peers = send.shape
    total = each * peers
    pick = one_hot(iota((total, peers), 0) // each == iota((total, peers), 1))
    full = dot(pick, narrow(send >> 5), NT) * 32.0 + dot(pick, narrow(send & 31), NT)
    mine = jnp.where(iota((total, each), 1) == iota((total, each), 0) % each, full, 0.0)
    return jnp.sum(mine, axis=1, keepdims=True).astype(jnp.int32)


def index_row(send):
    each, peers = send.shape
    total = each * peers
    pick = one_hot(iota((peers, total), 1) // each == iota((peers, total), 0))
    full = dot(narrow(send >> 5), pick) * 32.0 + dot(narrow(send & 31), pick)
    mine = jnp.where(iota((each, total), 0) == iota((each, total), 1) % each, full, 0.0)
    return jnp.sum(mine, axis=0, keepdims=True).astype(jnp.int32)


def gather_matrix(column, rows):
    return one_hot(iota((column.shape[0], rows), 1) == column)


def scatter_matrix(row, rows, first=0):
    return one_hot(iota((rows, row.shape[1]), 0) + first == row)


def put_pieces(ref, number, rows):
    ref[:, number * TILE : (number + 1) * TILE, :] = rows.reshape(ref.shape[0], TILE, ref.shape[2])


def get_pieces(ref, number):
    return ref[:, number * TILE : (number + 1) * TILE, :].reshape(ref.shape[0] * TILE, ref.shape[2])


class Far:
    def __init__(self, source, here, sem):
        self.here = here
        self.copy = pltpu.make_async_copy(source, here, sem)
        self.shape = here.shape
        self.copy.start()
        self.waiting = True

    def __getitem__(self, at):
        if self.waiting:
            self.copy.wait()
            self.waiting = False
        return self.here[at]


class FarOut:
    def __init__(self, target, here, sem):
        self.here = here
        self.copy = pltpu.make_async_copy(here, target, sem)
        self.shape = here.shape

    def __setitem__(self, at, value):
        self.here[at] = value

    def __getitem__(self, at):
        return self.here[at]

    def send(self):
        self.copy.start()


def sds(shape, dtype):
    return jax.ShapeDtypeStruct(shape, dtype)


def call(body, out, args, where, flops=0, name=None, room=ROOM):
    many = isinstance(out, tuple)
    outs = out if many else (out,)
    every = list(args) + list(outs)
    spaces, staged, shapes = [], [], []
    for value, mark in zip(every, where, strict=True):
        if mark == "v":
            spaces.append(pl.BlockSpec(memory_space=pltpu.VMEM))
        elif mark == "x":
            spaces.append(pl.BlockSpec(memory_space=pl.ANY))
        elif mark == "s":
            spaces.append(pl.BlockSpec(memory_space=pltpu.SMEM))
        else:
            spaces.append(pl.BlockSpec(memory_space=pltpu.HBM))
            shape = value.shape if mark == "f" else (mark,) + value.shape[1:]
            shapes.append(pltpu.VMEM(shape, value.dtype))
        staged.append(mark not in ("v", "s", "x"))
    count = len(shapes)

    def kernel(*refs):
        given = list(refs[: len(every)])
        scratch = list(refs[len(every) : len(every) + count])
        sems = refs[-1] if count else None
        used = 0
        late = []
        for k, far in enumerate(staged):
            if not far:
                continue
            here = scratch[used]
            if k < len(args):
                source = given[k] if where[k] == "f" else given[k].at[pl.ds(0, where[k])]
                given[k] = Far(source, here, sems.at[used])
            else:
                given[k] = FarOut(given[k], here, sems.at[used])
                late.append(given[k])
            used += 1
        body(*given)
        for item in given[: len(args)]:
            if isinstance(item, Far) and item.waiting:
                item.copy.wait()
        for item in late:
            item.copy.wait()

    moved = sum(v.size * v.dtype.itemsize for v in every)
    return pl.pallas_call(
        kernel,
        out_shape=out,
        in_specs=spaces[: len(args)],
        out_specs=tuple(spaces[len(args) :]) if many else spaces[-1],
        scratch_shapes=shapes + ([pltpu.SemaphoreType.DMA((count,))] if count else []),
        compiler_params=pltpu.CompilerParams(vmem_limit_bytes=room),
        cost_estimate=pl.CostEstimate(flops=flops, bytes_accessed=moved, transcendentals=0),
        name=name,
    )(*args)


def first_kernel(send, x, d, o):
    chosen = gather_matrix(index_column(send[...]), x.shape[0])
    put_pieces(o, 1, d[...])
    put_pieces(o, 0, dot(chosen, x[...]).astype(BF16))


def adjacency_kernel(counts, ib, ob, it, ot, x, master, mirror, part_master, part_mirror, mirror_mirror):
    masters = x.shape[0] // BLOCK
    mirrors = mirror.shape[1] // BLOCK
    master.here[...] = jnp.zeros(master.shape, BF16)
    mirror.here[...] = jnp.zeros(mirror.shape, BF16)

    def place(tiles, table, count, into, first):
        def step(k, carry):
            @pl.when(k < count)
            def _():
                dst = table[0, k]
                dst = jnp.where(dst >= masters, dst - masters, dst + mirrors)
                src = table[1, k] - first
                rows = pl.ds(pl.multiple_of(dst * BLOCK, BLOCK), BLOCK)
                cols = pl.ds(pl.multiple_of(src * BLOCK, BLOCK), BLOCK)
                into[rows, cols] = tiles[k]

            return carry

        lax.fori_loop(0, tiles.shape[0], step, 0)

    it.copy.wait()
    it.waiting = False
    ot.copy.wait()
    ot.waiting = False
    place(it.here, ib, counts[0, 0], master.here, 0)
    place(ot.here, ob, counts[0, 1], mirror.here, masters)
    master.send()
    mirror.send()
    size = mirrors * BLOCK
    mirror_mirror[...] = mirror[:size, :]
    part_mirror[...] = dot(master[:size, :], x[...])
    part_master[...] = dot(master[size:, :], x[...])
    part_master.send()


def mirror_part_kernel(part, a, got, o):
    rows = part[...] + dot(a[...], get_pieces(got, 0))
    put_pieces(o, 0, rows.astype(BF16))


def master_part_kernel(part, a, got, x, w, send, d, p, z, g):
    m = a.shape[1]
    z[...] = dot(x[...], w[...])
    z.send()
    p[...] = part[...] + dot(a[m:, :], get_pieces(got, 0))
    p.send()
    spread = scatter_matrix(index_row(send[...]), x.shape[0])
    g[...] = d[...].astype(F32) + dot(spread, get_pieces(got, 1))
    g.send()


def dense_kernel(send, deg, p, z, g, got, w, avg, out, dz, davg, pick):
    rows = p.shape[0]
    spread = scatter_matrix(index_row(send[...]), rows)
    chosen = gather_matrix(index_column(send[...]), rows)
    collected = dot(spread, get_pieces(got, 0))
    share = 1.0 / deg[...]
    mean = ((p[...] + collected) * share).astype(BF16)
    avg[...] = mean
    avg.send()
    zz = z[...] + dot(mean, w[...])
    s = jax.nn.sigmoid(zz)
    u = zz * s
    scale = lax.rsqrt(jnp.mean(u * u, axis=1, keepdims=True) + 1e-05)
    n = u * scale
    out[...] = n.astype(BF16)
    out.send()
    gg = g[...]
    du = scale * (gg - n * jnp.mean(gg * n, axis=1, keepdims=True))
    dz[...] = (du * (s + u * (1.0 - s))).astype(BF16)
    dz.send()
    davg[...] = (dot(dz[...], w[...], NT) * share).astype(BF16)
    davg.send()
    put_pieces(pick, 0, dot(chosen, davg[...]).astype(BF16))
    put_pieces(pick, 1, dot(chosen, out[...]).astype(BF16))


def weight_kernel(x, avg, dz, after, o):
    half = o.shape[0] // 2
    put_pieces(o.at[:half], 0, dot(x[...], dz[...], TN).astype(BF16))
    put_pieces(o.at[half:], 0, dot(avg[...], dz[...], TN).astype(BF16))


def back_kernel(dz, w, davg, am, ar, o, r):
    m = ar.shape[1]
    r[...] = dot(ar[m:, :], davg[...], TN)
    o[...] = dot(dz[...], w[...], NT) + dot(am[m:, :], davg[...], TN)
    o.send()


def mirror_back_kernel(back, a, got, o):
    put_pieces(o, 0, (back[...] + dot(a[...], get_pieces(got, 0), TN)).astype(BF16))


def master_back_kernel(back, a, got, o, out):
    o[...] = back[...] + dot(a[...], get_pieces(got, 0), TN)
    o.send()
    out[...] = get_pieces(got, 1)
    out.send()


def pack_kernel(rows, got, o):
    o[:, :TILE, :] = rows[...]
    total = jnp.sum(got[...].astype(F32), axis=0).astype(BF16)
    o[:, TILE:, :] = jnp.broadcast_to(total[None], (o.shape[0],) + total.shape)


def share_kernel(got, o):
    total = jnp.sum(got[:, TILE:, :].astype(F32), axis=0).astype(BF16)
    o[...] = jnp.broadcast_to(total[None], o.shape)


def grad_kernel(send, back, got, o):
    spread = scatter_matrix(index_row(send[...]), o.shape[0])
    o[...] = (back[...] + dot(spread, get_pieces(got, 0))).astype(BF16)
    o.send()


def widen_kernel(got, w_self, w_neigh):
    half = got.shape[0] // 2
    w_self[...] = get_pieces(got.at[:half], 0).astype(F32)
    w_self.send()
    w_neigh[...] = get_pieces(got.at[half:], 0).astype(F32)
    w_neigh.send()


def on_device(
    dom,
    grp,
    features,
    w_self,
    w_neigh,
    degree,
    send_rows,
    inner_tiles,
    inner_blocks,
    outer_tiles,
    outer_blocks,
    tile_counts,
    d_out,
    d_mirror,
):
    rows, width = features.shape
    peers, each = send_rows.shape
    mirrors = peers * each
    slots = rows + mirrors
    mm = 2 * width
    groups = lax.axis_size(grp)
    def exchange(values, axis):
        return lax.all_to_all(values, axis, split_axis=0, concat_axis=0, tiled=True)

    def parcel(count, many=peers):
        return sds((many, count * TILE, width), BF16)

    def wide(count, dtype=F32):
        return sds((count, width), dtype)

    send = send_rows.T
    degree_col = degree[:, None]

    got_h = exchange(
        call(first_kernel, parcel(2), (send, features, d_mirror), "vffv", mm * mirrors * rows, "pick_h"), dom
    )
    a_master, a_mirror, part_master, part_mirror, a_corner = call(
        adjacency_kernel,
        (sds((slots, rows), BF16), sds((slots, mirrors), BF16), wide(rows), wide(mirrors), sds((mirrors, mirrors), BF16)),
        (tile_counts, inner_blocks.T, outer_blocks.T, inner_tiles, outer_tiles, features),
        "sss" + "fff" + "fffvv",
        mm * slots * rows,
        "adjacency",
        40000000,
    )
    mirror_part = call(
        mirror_part_kernel, parcel(1), (part_mirror, a_corner, got_h), "vvvv", mm * mirrors * mirrors, "mirror_part", LITTLE
    )
    got_part = exchange(mirror_part, dom)
    p_master, z_self, g_out = call(
        master_part_kernel,
        (wide(rows),) * 3,
        (part_master, a_mirror, got_h, features, w_self, send, d_out),
        "ffvfvvf" + "fff",
        mm * rows * (2 * mirrors + width),
        "master_part",
    )
    avg, out, dz, d_avg, pick_g = call(
        dense_kernel,
        (wide(rows, BF16),) * 4 + (parcel(2),),
        (send, degree_col, p_master, z_self, g_out, got_part, w_neigh),
        "vffffvv" + "ffffv",
        mm * rows * (2 * mirrors + 2 * width),
        "dense",
    )
    got_g = exchange(pick_g, dom)
    back, back_mirror = call(
        back_kernel,
        (wide(rows), wide(mirrors)),
        (dz, w_self, d_avg, a_master, a_mirror),
        "fvfff" + "fv",
        mm * rows * (width + slots),
        "back",
    )
    terms = call(
        weight_kernel, parcel(1, groups), (features, avg, dz, back_mirror), "fff" + "x" + "v", 2 * mm * rows * width, "weights"
    )
    got_terms = exchange(terms, grp)
    mirror_back = call(
        mirror_back_kernel,
        parcel(1),
        (back_mirror, a_corner, got_g),
        "vvvv",
        mm * mirrors * mirrors,
        "mirror_back",
        LITTLE,
    )
    packed = call(pack_kernel, parcel(2), (mirror_back, got_terms), "vvv", 0, "pack", LITTLE)
    got_back = exchange(packed, dom)
    back, mirror_out = call(
        master_back_kernel,
        (wide(rows), wide(mirrors, BF16)),
        (back, a_master, got_g),
        ("f", mirrors, "v", "f", "f"),
        mm * rows * mirrors,
        "master_back",
    )
    shared = call(share_kernel, parcel(1, groups), (got_back,), "vv", 0, "share", LITTLE)
    totals = exchange(shared, grp)
    grad_h = call(
        grad_kernel, wide(rows, BF16), (send, back, got_back), "vfv" + "f", mm * rows * mirrors, "grad"
    )
    grad_wself, grad_wneigh = call(
        widen_kernel, (wide(width),) * 2, (totals,), "vff", 0, "widen", LITTLE
    )
    return (out, mirror_out, grad_h, grad_wself, grad_wneigh)


def solution(mesh):
    names = ("dom", "grp")
    split = lambda rank: P(names, *([None] * (rank - 1)))
    in_specs = (
        split(2), P(), P(), split(1), split(2), split(3), split(2), split(3), split(2), split(2),
        split(2), split(2),
    )
    out_specs = (split(2), split(2), split(2), P(), P())
    return jax.shard_map(
        functools.partial(on_device, "dom", "grp"),
        mesh=mesh, in_specs=in_specs, out_specs=out_specs, check_vma=False,
    )
```

profile of v0, /device:TPU:8, one launch (start us, length us, event | category | flops | bytes accessed | tf_op | source)
XLA Modules:
  0.0 153.9 jit_solution(5059277386180843761)
XLA Ops:
  0.6 0.0 copy-start.14
  0.6 2.9 %pick_h.1 = bf16[24,32,256]{2,1,0:T(8,128)(2,1)} custom-call(s32[16,24]{1,0:T(8,128)} %bitcast.6, bf16[1024,256]{1,0:T(8,128)(2,1)} %refs_0_.3, bf16[384,256]{1,0:T(8,128)(2,1)} %refs_2_.1), custom_call_target="tpu_custom_call" | custom-call | flops 201326592 | bytes 1115648 | tf_op jit(solution)/shard_map/pick_h/pallas_call | solution.py:150
  3.6 15.4 %all-to-all-start = ((bf16[24,32,256]{2,1,0:T(8,128)(2,1)}), bf16[24,32,256]{2,1,0:T(8,128)(2,1)S(1)}, u32[]{:S(2)}, u32[]{:S(2)}) async-start(bf16[24,32,256]{2,1,0:T(8,128)(2,1)} %pick_h.1), calls=%async_computation | async-start | bytes 786432 | tf_op jit(solution)/shard_map/all_to_all | solution.py:318
  19.0 0.0 copy-start.1
  19.0 1.0 copy-done.1
  20.0 0.0 copy-start.8
  20.0 1.2 copy-done.8
  21.2 0.0 copy-start.9
  21.2 1.0 copy-done.9
  22.2 0.0 copy-start.10
  22.2 0.7 copy-done.10
  22.9 0.0 copy-start.11
  22.9 0.7 copy-done.11
  23.6 0.0 copy-start.12
  23.6 0.7 copy-done.12
  24.2 3.6 %adjacency.1 = (bf16[1408,1024]{1,0:T(8,128)(2,1)S(1)}, bf16[1408,384]{1,0:T(8,128)(2,1)S(1)}, f32[1024,256]{1,0:T(8,128)S(1)}, f32[384,256]{1,0:T(8,128)S(1)}, bf16[384,384]{1,0:T(8,128)(2,1)S(1)}) custom-call(s32[1,2]{1,0:T(1,128)S(1)} %copy-done.12, s32[2,26]{1,0:T(2,128)S(1)} %bitcast.4, s32[2,15]{1,0:T(2,128)S(1)} %bitcast.5, ...), custom_call_target="tpu_custom_call" | custom-call | flops 738197504 | bytes 7569744 | tf_op jit(solution)/shard_map/adjacency/pallas_call | solution.py:150
  27.8 0.0 copy-start
  27.8 1.5 %copy-done = bf16[1408,1024]{1,0:T(8,128)(2,1)} copy-done((bf16[1408,1024]{1,0:T(8,128)(2,1)}, bf16[1408,1024]{1,0:T(8,128)(2,1)S(1)}, u32[]{:S(2)}) %copy-start) | copy-done | bytes 2883608
  29.3 0.0 copy-start.2
  29.3 1.0 copy-done.2
  30.4 0.0 copy-start.7
  30.4 1.0 copy-done.7
  31.4 8.3 %all-to-all-done.refs_2_ = bf16[24,32,256]{2,1,0:T(8,128)(2,1)S(1)} async-done(((bf16[24,32,256]{2,1,0:T(8,128)(2,1)}), bf16[24,32,256]{2,1,0:T(8,128)(2,1)S(1)}, u32[]{:S(2)}, u32[]{:S(2)}) %all-to-all-start) | async-done | bytes 393248 | tf_op jit(solution)/shard_map/all_to_all | solution.py:318
  39.7 0.0 copy-start.4
  39.7 0.9 mirror_part.1
  40.6 3.8 %all-to-all-start.1 = ((bf16[24,16,256]{2,1,0:T(8,128)(2,1)}), bf16[24,16,256]{2,1,0:T(8,128)(2,1)S(1)}, u32[]{:S(2)}, u32[]{:S(2)}) async-start(bf16[24,16,256]{2,1,0:T(8,128)(2,1)} %mirror_part.1), calls=%async_computation.1 | async-start | bytes 393216 | tf_op jit(solution)/shard_map/all_to_all | solution.py:318
  44.5 0.0 copy-done.14
  44.5 1.0 copy.17.refs_1_
  45.5 0.0 copy-done.4
  45.5 5.7 %master_part.1 = (f32[1024,256]{1,0:T(8,128)}, f32[1024,256]{1,0:T(8,128)}, f32[1024,256]{1,0:T(8,128)}) custom-call(f32[1024,256]{1,0:T(8,128)} %copy-done.7, bf16[1408,384]{1,0:T(8,128)(2,1)} %copy-done.2, bf16[24,32,256]{2,1,0:T(8,128)(2,1)} %copy-done.4, bf16[1024,256]{1,0:T(8,128)(2,1)} %refs_0_.3, bf16[256,256]{1,0:T(8,128)(2,1)} %refs_1_.3, ...), custom_call_target="tpu_custom_call" | custom-call | flops 536870912 | bytes 6850048 | tf_op jit(solution)/shard_map/master_part/pallas_call | solution.py:150
  51.2 7.9 %all-to-all-done.1.refs_5_ = bf16[24,16,256]{2,1,0:T(8,128)(2,1)S(1)} async-done(((bf16[24,16,256]{2,1,0:T(8,128)(2,1)}), bf16[24,16,256]{2,1,0:T(8,128)(2,1)S(1)}, u32[]{:S(2)}, u32[]{:S(2)}) %all-to-all-start.1) | async-done | bytes 196640 | tf_op jit(solution)/shard_map/all_to_all | solution.py:318
  59.1 0.0 copy-start.13
  59.1 0.7 copy-done.13
  59.8 5.6 %dense.1 = (bf16[1024,256]{1,0:T(8,128)(2,1)}, bf16[1024,256]{1,0:T(8,128)(2,1)}, bf16[1024,256]{1,0:T(8,128)(2,1)}, bf16[1024,256]{1,0:T(8,128)(2,1)}, bf16[24,32,256]{2,1,0:T(8,128)(2,1)}) custom-call(s32[16,24]{1,0:T(8,128)} %bitcast.8, f32[1024,1]{1,0:T(8,128)} %copy.17.refs_1_, f32[1024,256]{1,0:T(8,128)} %get-tuple-element.26.refs_2_, ...), custom_call_target="tpu_custom_call" | custom-call | flops 671088640 | bytes 5969408 | tf_op jit(solution)/shard_map/dense/pallas_call | solution.py:150
  65.4 3.9 %all-to-all-start.2 = ((bf16[24,32,256]{2,1,0:T(8,128)(2,1)}), bf16[24,32,256]{2,1,0:T(8,128)(2,1)S(1)}, u32[]{:S(2)}, u32[]{:S(2)}) async-start(bf16[24,32,256]{2,1,0:T(8,128)(2,1)} %get-tuple-element.36), calls=%async_computation.2 | async-start | bytes 786432 | tf_op jit(solution)/shard_map/all_to_all | solution.py:318
  69.3 6.9 %back.1 = (f32[1024,256]{1,0:T(8,128)}, f32[384,256]{1,0:T(8,128)}) custom-call(bf16[1024,256]{1,0:T(8,128)(2,1)} %get-tuple-element.32.refs_0_.refs_2_, bf16[256,256]{1,0:T(8,128)(2,1)} %refs_1_.3, bf16[1024,256]{1,0:T(8,128)(2,1)} %get-tuple-element.33.refs_2_, bf16[1408,1024]{1,0:T(8,128)(2,1)} %copy-done, bf16[1408,384]{1,0:T(8,128)(2,1)} %copy-done.2), custom_call_target="tpu_custom_call" | custom-call | flops 872415232 | bytes 6586368 | tf_op jit(solution)/shard_map/back/pallas_call | solution.py:150
  76.2 0.0 copy-start.6
  76.2 3.0 %weights.1 = bf16[32,16,256]{2,1,0:T(8,128)(2,1)} custom-call(bf16[1024,256]{1,0:T(8,128)(2,1)} %refs_0_.3, bf16[1024,256]{1,0:T(8,128)(2,1)} %get-tuple-element.40.refs_1_, bf16[1024,256]{1,0:T(8,128)(2,1)} %get-tuple-element.32.refs_0_.refs_2_, f32[384,256]{1,0:T(8,128)} %get-tuple-element.39.refs_0_.refs_3_), custom_call_target="tpu_custom_call" | custom-call | flops 268435456 | bytes 2228224 | tf_op jit(solution)/shard_map/weights/pallas_call | solution.py:150
  79.2 10.8 %all-to-all-done.2.refs_2_ = bf16[24,32,256]{2,1,0:T(8,128)(2,1)S(1)} async-done(((bf16[24,32,256]{2,1,0:T(8,128)(2,1)}), bf16[24,32,256]{2,1,0:T(8,128)(2,1)S(1)}, u32[]{:S(2)}, u32[]{:S(2)}) %all-to-all-start.2) | async-done | bytes 393248 | tf_op jit(solution)/shard_map/all_to_all | solution.py:318
  90.0 0.0 copy-start.3
  90.0 10.2 %all-to-all-start.3 = ((bf16[32,16,256]{2,1,0:T(8,128)(2,1)}), bf16[32,16,256]{2,1,0:T(8,128)(2,1)S(1)}, u32[]{:S(2)}, u32[]{:S(2)}) async-start(bf16[32,16,256]{2,1,0:T(8,128)(2,1)} %weights.1), calls=%async_computation.3 | async-start | bytes 524288 | tf_op jit(solution)/shard_map/all_to_all | solution.py:318
  100.1 0.0 copy-done.6
  100.2 0.3 mirror_back.1.refs_0_
  100.5 10.8 %all-to-all-done.3.refs_1_ = bf16[32,16,256]{2,1,0:T(8,128)(2,1)S(1)} async-done(((bf16[32,16,256]{2,1,0:T(8,128)(2,1)}), bf16[32,16,256]{2,1,0:T(8,128)(2,1)S(1)}, u32[]{:S(2)}, u32[]{:S(2)}) %all-to-all-start.3) | async-done | bytes 262176 | tf_op jit(solution)/shard_map/all_to_all | solution.py:318
  111.2 0.1 pack.1
  111.3 25.3 %all_to_all.30.refs_2_.refs_0_ = bf16[24,32,256]{2,1,0:T(8,128)(2,1)S(1)} all-to-all(bf16[24,32,256]{2,1,0:T(8,128)(2,1)S(1)} %pack.1), channel_id=1, replica_groups=mesh['dom'=24,'grp'=32] {'dom'}, dimensions={0} | all-to-all | bytes 786432 | tf_op jit(solution)/shard_map/all_to_all | solution.py:318
  136.6 0.0 copy-start.5
  136.6 0.8 share.1
  137.4 4.6 %all-to-all-start.5 = ((bf16[32,16,256]{2,1,0:T(8,128)(2,1)}), bf16[32,16,256]{2,1,0:T(8,128)(2,1)S(1)}, u32[]{:S(2)}, u32[]{:S(2)}) async-start(bf16[32,16,256]{2,1,0:T(8,128)(2,1)} %share.1), calls=%async_computation.5 | async-start | bytes 524288 | tf_op jit(solution)/shard_map/all_to_all | solution.py:318
  141.9 0.0 copy-done.3
  142.0 4.0 %master_back.1 = (f32[1024,256]{1,0:T(8,128)}, bf16[384,256]{1,0:T(8,128)(2,1)}) custom-call(f32[1024,256]{1,0:T(8,128)} %get-tuple-element.35.refs_0_, bf16[1408,1024]{1,0:T(8,128)(2,1)} %copy-done, bf16[24,32,256]{2,1,0:T(8,128)(2,1)} %copy-done.3), custom_call_target="tpu_custom_call" | custom-call | flops 201326592 | bytes 5570560 | tf_op jit(solution)/shard_map/master_back/pallas_call | solution.py:150
  145.9 0.0 copy-done.5
  146.0 3.5 %grad.1 = bf16[1024,256]{1,0:T(8,128)(2,1)} custom-call(s32[16,24]{1,0:T(8,128)} %bitcast.9, f32[1024,256]{1,0:T(8,128)} %get-tuple-element.38.refs_1_, bf16[24,32,256]{2,1,0:T(8,128)(2,1)} %copy-done.5), custom_call_target="tpu_custom_call" | custom-call | flops 201326592 | bytes 1967616 | tf_op jit(solution)/shard_map/grad/pallas_call | solution.py:150
  149.4 3.6 %all-to-all-done.5.refs_0_ = bf16[32,16,256]{2,1,0:T(8,128)(2,1)S(1)} async-done(((bf16[32,16,256]{2,1,0:T(8,128)(2,1)}), bf16[32,16,256]{2,1,0:T(8,128)(2,1)S(1)}, u32[]{:S(2)}, u32[]{:S(2)}) %all-to-all-start.5) | async-done | bytes 262176 | tf_op jit(solution)/shard_map/all_to_all | solution.py:318
  153.0 0.8 widen.1
Async XLA Ops:
  0.6 43.8 %copy-start.14 = (f32[1024]{0:T(1024)S(1)}, f32[1024]{0:T(1024)}, u32[]{:S(2)}) copy-start(f32[1024]{0:T(1024)} %param.15) | copy-start | bytes 12292
  3.6 36.1 %all-to-all-start = ((bf16[24,32,256]{2,1,0:T(8,128)(2,1)}), bf16[24,32,256]{2,1,0:T(8,128)(2,1)S(1)}, u32[]{:S(2)}, u32[]{:S(2)}) async-start(bf16[24,32,256]{2,1,0:T(8,128)(2,1)} %pick_h.1), calls=%async_computation | async-start | bytes 786432 | tf_op jit(solution)/shard_map/all_to_all | solution.py:318
  19.0 1.0 copy-start.1
  20.0 1.2 copy-start.8
  21.2 1.0 copy-start.9
  22.2 0.7 copy-start.10
  22.9 0.7 copy-start.11
  23.6 0.7 copy-start.12
  27.8 1.6 %copy-start = (bf16[1408,1024]{1,0:T(8,128)(2,1)}, bf16[1408,1024]{1,0:T(8,128)(2,1)S(1)}, u32[]{:S(2)}) copy-start(bf16[1408,1024]{1,0:T(8,128)(2,1)S(1)} %get-tuple-element.34.refs_3_.refs_1_) | copy-start | bytes 8650756
  29.3 1.0 copy-start.2
  30.4 1.0 copy-start.7
  39.7 5.8 %copy-start.4 = (bf16[24,32,256]{2,1,0:T(8,128)(2,1)}, bf16[24,32,256]{2,1,0:T(8,128)(2,1)S(1)}, u32[]{:S(2)}) copy-start(bf16[24,32,256]{2,1,0:T(8,128)(2,1)S(1)} %all-to-all-done.refs_2_) | copy-start | bytes 1179652
  40.6 18.5 %all-to-all-start.1 = ((bf16[24,16,256]{2,1,0:T(8,128)(2,1)}), bf16[24,16,256]{2,1,0:T(8,128)(2,1)S(1)}, u32[]{:S(2)}, u32[]{:S(2)}) async-start(bf16[24,16,256]{2,1,0:T(8,128)(2,1)} %mirror_part.1), calls=%async_computation.1 | async-start | bytes 393216 | tf_op jit(solution)/shard_map/all_to_all | solution.py:318
  59.1 0.7 copy-start.13
  65.4 24.6 %all-to-all-start.2 = ((bf16[24,32,256]{2,1,0:T(8,128)(2,1)}), bf16[24,32,256]{2,1,0:T(8,128)(2,1)S(1)}, u32[]{:S(2)}, u32[]{:S(2)}) async-start(bf16[24,32,256]{2,1,0:T(8,128)(2,1)} %get-tuple-element.36), calls=%async_computation.2 | async-start | bytes 786432 | tf_op jit(solution)/shard_map/all_to_all | solution.py:318
  76.2 24.0 %copy-start.6 = (f32[384,256]{1,0:T(8,128)S(1)}, f32[384,256]{1,0:T(8,128)}, u32[]{:S(2)}) copy-start(f32[384,256]{1,0:T(8,128)} %get-tuple-element.39.refs_0_.refs_3_) | copy-start | bytes 1179652
  90.0 52.0 %copy-start.3 = (bf16[24,32,256]{2,1,0:T(8,128)(2,1)}, bf16[24,32,256]{2,1,0:T(8,128)(2,1)S(1)}, u32[]{:S(2)}) copy-start(bf16[24,32,256]{2,1,0:T(8,128)(2,1)S(1)} %all-to-all-done.2.refs_2_) | copy-start | bytes 1179652
  90.0 21.3 %all-to-all-start.3 = ((bf16[32,16,256]{2,1,0:T(8,128)(2,1)}), bf16[32,16,256]{2,1,0:T(8,128)(2,1)S(1)}, u32[]{:S(2)}, u32[]{:S(2)}) async-start(bf16[32,16,256]{2,1,0:T(8,128)(2,1)} %weights.1), calls=%async_computation.3 | async-start | bytes 524288 | tf_op jit(solution)/shard_map/all_to_all | solution.py:318
  136.6 9.4 %copy-start.5 = (bf16[24,32,256]{2,1,0:T(8,128)(2,1)}, bf16[24,32,256]{2,1,0:T(8,128)(2,1)S(1)}, u32[]{:S(2)}) copy-start(bf16[24,32,256]{2,1,0:T(8,128)(2,1)S(1)} %all_to_all.30.refs_2_.refs_0_) | copy-start | bytes 1179652
  137.4 15.7 %all-to-all-start.5 = ((bf16[32,16,256]{2,1,0:T(8,128)(2,1)}), bf16[32,16,256]{2,1,0:T(8,128)(2,1)S(1)}, u32[]{:S(2)}, u32[]{:S(2)}) async-start(bf16[32,16,256]{2,1,0:T(8,128)(2,1)} %share.1), calls=%async_computation.5 | async-start | bytes 524288 | tf_op jit(solution)/shard_map/all_to_all | solution.py:318
where the time goes:
time: 155 us; the launch traced here: 154 us
  waiting for transfers between devices  41.3 us (27%)
  Pallas kernels  38.1 us (25%)
  starting transfers between devices  37.8 us (24%)
  blocking collectives  25.3 us (16%)
  local copies, waits for them, and re-layouts  10.6 us (7%)
    all_to_all x5, waiting for transfers between devices, exchange(): return lax.all_to_all(values, axis, split_axis=0, concat_axis=0, tiled=True)  41.3 us
    pallas_call x13, Pallas kernels, call(): pl.pallas_call(kernel, out_shape=out, in_specs=spaces[:len(args)], out_sp...  38.1 us
    all_to_all x5, starting transfers between devices, exchange(): return lax.all_to_all(values, axis, split_axis=0, concat_axis=0, tiled=True)  37.8 us
    all_to_all x1, blocking collectives, exchange(): return lax.all_to_all(values, axis, split_axis=0, concat_axis=0, tiled=True)  25.3 us
    unnamed x30, local copies, waits for them, and re-layouts  9.54 us
  transfers between devices with their start and end apart: 5, of which 5 were waited for; matrix products, arithmetic and copies ran while one was open for 1% of the time, Pallas kernels for 17%

commit v1 on v0

--- a/solution.py
+++ b/solution.py
@@ -233,6 +233,7 @@
     n = u * scale
     out[...] = n.astype(BF16)
     out.send()
+    put_pieces(pick, 1, dot(chosen, out[...]).astype(BF16))
     gg = g[...]
     du = scale * (gg - n * jnp.mean(gg * n, axis=1, keepdims=True))
     dz[...] = (du * (s + u * (1.0 - s))).astype(BF16)
@@ -240,7 +241,6 @@
     davg[...] = (dot(dz[...], w[...], NT) * share).astype(BF16)
     davg.send()
     put_pieces(pick, 0, dot(chosen, davg[...]).astype(BF16))
-    put_pieces(pick, 1, dot(chosen, out[...]).astype(BF16))
 
 
 def weight_kernel(x, avg, dz, after, o):

time: 155 us -> 155 us (level)
  no operation moved by 1% of the time
where the time goes in v1:
time: 155 us; the launch traced here: 154 us
  waiting for transfers between devices  41.4 us (27%)
  Pallas kernels  38.4 us (25%)
  starting transfers between devices  37.8 us (24%)
  blocking collectives  25.3 us (16%)
  local copies, waits for them, and re-layouts  10.6 us (7%)
    all_to_all x5, waiting for transfers between devices, exchange(): return lax.all_to_all(values, axis, split_axis=0, concat_axis=0, tiled=True)  41.4 us
    pallas_call x13, Pallas kernels, call(): pl.pallas_call(kernel, out_shape=out, in_specs=spaces[:len(args)], out_sp...  38.4 us
    all_to_all x5, starting transfers between devices, exchange(): return lax.all_to_all(values, axis, split_axis=0, concat_axis=0, tiled=True)  37.8 us
    all_to_all x1, blocking collectives, exchange(): return lax.all_to_all(values, axis, split_axis=0, concat_axis=0, tiled=True)  25.3 us
    unnamed x30, local copies, waits for them, and re-layouts  9.54 us
  transfers between devices with their start and end apart: 5, of which 5 were waited for; matrix products, arithmetic and copies ran while one was open for 1% of the time, Pallas kernels for 17%

profile of v1, /device:TPU:8, one launch (start us, length us, event | category | flops | bytes accessed | tf_op | source)
XLA Modules:
  0.0 154.3 jit_solution(8517837045098685467)
XLA Ops:
  0.6 0.0 copy-start.14
  0.6 2.9 %pick_h.1 = bf16[24,32,256]{2,1,0:T(8,128)(2,1)} custom-call(s32[16,24]{1,0:T(8,128)} %bitcast.6, bf16[1024,256]{1,0:T(8,128)(2,1)} %refs_0_.3, bf16[384,256]{1,0:T(8,128)(2,1)} %refs_2_.1), custom_call_target="tpu_custom_call" | custom-call | flops 201326592 | bytes 1115648 | tf_op jit(solution)/shard_map/pick_h/pallas_call | solution.py:150
  3.6 15.4 %all-to-all-start = ((bf16[24,32,256]{2,1,0:T(8,128)(2,1)}), bf16[24,32,256]{2,1,0:T(8,128)(2,1)S(1)}, u32[]{:S(2)}, u32[]{:S(2)}) async-start(bf16[24,32,256]{2,1,0:T(8,128)(2,1)} %pick_h.1), calls=%async_computation | async-start | bytes 786432 | tf_op jit(solution)/shard_map/all_to_all | solution.py:318
  19.0 0.0 copy-start.1
  19.0 1.0 copy-done.1
  20.0 0.0 copy-start.8
  20.0 1.2 copy-done.8
  21.2 0.0 copy-start.9
  21.2 1.0 copy-done.9
  22.2 0.0 copy-start.10
  22.2 0.7 copy-done.10
  22.9 0.0 copy-start.11
  22.9 0.7 copy-done.11
  23.6 0.0 copy-start.12
  23.6 0.7 copy-done.12
  24.2 3.4 %adjacency.1 = (bf16[1408,1024]{1,0:T(8,128)(2,1)S(1)}, bf16[1408,384]{1,0:T(8,128)(2,1)S(1)}, f32[1024,256]{1,0:T(8,128)S(1)}, f32[384,256]{1,0:T(8,128)S(1)}, bf16[384,384]{1,0:T(8,128)(2,1)S(1)}) custom-call(s32[1,2]{1,0:T(1,128)S(1)} %copy-done.12, s32[2,26]{1,0:T(2,128)S(1)} %bitcast.4, s32[2,15]{1,0:T(2,128)S(1)} %bitcast.5, ...), custom_call_target="tpu_custom_call" | custom-call | flops 738197504 | bytes 7569744 | tf_op jit(solution)/shard_map/adjacency/pallas_call | solution.py:150
  27.7 0.0 copy-start
  27.7 1.5 %copy-done = bf16[1408,1024]{1,0:T(8,128)(2,1)} copy-done((bf16[1408,1024]{1,0:T(8,128)(2,1)}, bf16[1408,1024]{1,0:T(8,128)(2,1)S(1)}, u32[]{:S(2)}) %copy-start) | copy-done | bytes 2883608
  29.2 0.0 copy-start.2
  29.2 1.0 copy-done.2
  30.3 0.0 copy-start.7
  30.3 1.0 copy-done.7
  31.3 8.4 %all-to-all-done.refs_2_ = bf16[24,32,256]{2,1,0:T(8,128)(2,1)S(1)} async-done(((bf16[24,32,256]{2,1,0:T(8,128)(2,1)}), bf16[24,32,256]{2,1,0:T(8,128)(2,1)S(1)}, u32[]{:S(2)}, u32[]{:S(2)}) %all-to-all-start) | async-done | bytes 393248 | tf_op jit(solution)/shard_map/all_to_all | solution.py:318
  39.7 0.0 copy-start.4
  39.7 0.9 mirror_part.1
  40.6 3.8 %all-to-all-start.1 = ((bf16[24,16,256]{2,1,0:T(8,128)(2,1)}), bf16[24,16,256]{2,1,0:T(8,128)(2,1)S(1)}, u32[]{:S(2)}, u32[]{:S(2)}) async-start(bf16[24,16,256]{2,1,0:T(8,128)(2,1)} %mirror_part.1), calls=%async_computation.1 | async-start | bytes 393216 | tf_op jit(solution)/shard_map/all_to_all | solution.py:318
  44.5 0.0 copy-done.14
  44.5 1.0 copy.17.refs_1_
  45.5 0.0 copy-done.4
  45.5 5.7 %master_part.1 = (f32[1024,256]{1,0:T(8,128)}, f32[1024,256]{1,0:T(8,128)}, f32[1024,256]{1,0:T(8,128)}) custom-call(f32[1024,256]{1,0:T(8,128)} %copy-done.7, bf16[1408,384]{1,0:T(8,128)(2,1)} %copy-done.2, bf16[24,32,256]{2,1,0:T(8,128)(2,1)} %copy-done.4, bf16[1024,256]{1,0:T(8,128)(2,1)} %refs_0_.3, bf16[256,256]{1,0:T(8,128)(2,1)} %refs_1_.3, ...), custom_call_target="tpu_custom_call" | custom-call | flops 536870912 | bytes 6850048 | tf_op jit(solution)/shard_map/master_part/pallas_call | solution.py:150
  51.2 7.9 %all-to-all-done.1.refs_5_ = bf16[24,16,256]{2,1,0:T(8,128)(2,1)S(1)} async-done(((bf16[24,16,256]{2,1,0:T(8,128)(2,1)}), bf16[24,16,256]{2,1,0:T(8,128)(2,1)S(1)}, u32[]{:S(2)}, u32[]{:S(2)}) %all-to-all-start.1) | async-done | bytes 196640 | tf_op jit(solution)/shard_map/all_to_all | solution.py:318
  59.1 0.0 copy-start.13
  59.1 0.7 copy-done.13
  59.8 6.0 %dense.1 = (bf16[1024,256]{1,0:T(8,128)(2,1)}, bf16[1024,256]{1,0:T(8,128)(2,1)}, bf16[1024,256]{1,0:T(8,128)(2,1)}, bf16[1024,256]{1,0:T(8,128)(2,1)}, bf16[24,32,256]{2,1,0:T(8,128)(2,1)}) custom-call(s32[16,24]{1,0:T(8,128)} %bitcast.8, f32[1024,1]{1,0:T(8,128)} %copy.17.refs_1_, f32[1024,256]{1,0:T(8,128)} %get-tuple-element.26.refs_2_, ...), custom_call_target="tpu_custom_call" | custom-call | flops 671088640 | bytes 5969408 | tf_op jit(solution)/shard_map/dense/pallas_call | solution.py:150
  65.8 3.9 %all-to-all-start.2 = ((bf16[24,32,256]{2,1,0:T(8,128)(2,1)}), bf16[24,32,256]{2,1,0:T(8,128)(2,1)S(1)}, u32[]{:S(2)}, u32[]{:S(2)}) async-start(bf16[24,32,256]{2,1,0:T(8,128)(2,1)} %get-tuple-element.36), calls=%async_computation.2 | async-start | bytes 786432 | tf_op jit(solution)/shard_map/all_to_all | solution.py:318
  69.7 6.9 %back.1 = (f32[1024,256]{1,0:T(8,128)}, f32[384,256]{1,0:T(8,128)}) custom-call(bf16[1024,256]{1,0:T(8,128)(2,1)} %get-tuple-element.32.refs_0_.refs_2_, bf16[256,256]{1,0:T(8,128)(2,1)} %refs_1_.3, bf16[1024,256]{1,0:T(8,128)(2,1)} %get-tuple-element.33.refs_2_, bf16[1408,1024]{1,0:T(8,128)(2,1)} %copy-done, bf16[1408,384]{1,0:T(8,128)(2,1)} %copy-done.2), custom_call_target="tpu_custom_call" | custom-call | flops 872415232 | bytes 6586368 | tf_op jit(solution)/shard_map/back/pallas_call | solution.py:150
  76.6 0.0 copy-start.6
  76.6 3.0 %weights.1 = bf16[32,16,256]{2,1,0:T(8,128)(2,1)} custom-call(bf16[1024,256]{1,0:T(8,128)(2,1)} %refs_0_.3, bf16[1024,256]{1,0:T(8,128)(2,1)} %get-tuple-element.40.refs_1_, bf16[1024,256]{1,0:T(8,128)(2,1)} %get-tuple-element.32.refs_0_.refs_2_, f32[384,256]{1,0:T(8,128)} %get-tuple-element.39.refs_0_.refs_3_), custom_call_target="tpu_custom_call" | custom-call | flops 268435456 | bytes 2228224 | tf_op jit(solution)/shard_map/weights/pallas_call | solution.py:150
  79.6 10.8 %all-to-all-done.2.refs_2_ = bf16[24,32,256]{2,1,0:T(8,128)(2,1)S(1)} async-done(((bf16[24,32,256]{2,1,0:T(8,128)(2,1)}), bf16[24,32,256]{2,1,0:T(8,128)(2,1)S(1)}, u32[]{:S(2)}, u32[]{:S(2)}) %all-to-all-start.2) | async-done | bytes 393248 | tf_op jit(solution)/shard_map/all_to_all | solution.py:318
  90.4 0.0 copy-start.3
  90.4 10.2 %all-to-all-start.3 = ((bf16[32,16,256]{2,1,0:T(8,128)(2,1)}), bf16[32,16,256]{2,1,0:T(8,128)(2,1)S(1)}, u32[]{:S(2)}, u32[]{:S(2)}) async-start(bf16[32,16,256]{2,1,0:T(8,128)(2,1)} %weights.1), calls=%async_computation.3 | async-start | bytes 524288 | tf_op jit(solution)/shard_map/all_to_all | solution.py:318
  100.6 0.0 copy-done.6
  100.6 0.3 mirror_back.1.refs_0_
  100.9 10.8 %all-to-all-done.3.refs_1_ = bf16[32,16,256]{2,1,0:T(8,128)(2,1)S(1)} async-done(((bf16[32,16,256]{2,1,0:T(8,128)(2,1)}), bf16[32,16,256]{2,1,0:T(8,128)(2,1)S(1)}, u32[]{:S(2)}, u32[]{:S(2)}) %all-to-all-start.3) | async-done | bytes 262176 | tf_op jit(solution)/shard_map/all_to_all | solution.py:318
  111.7 0.1 pack.1
  111.7 25.3 %all_to_all.30.refs_2_.refs_0_ = bf16[24,32,256]{2,1,0:T(8,128)(2,1)S(1)} all-to-all(bf16[24,32,256]{2,1,0:T(8,128)(2,1)S(1)} %pack.1), channel_id=1, replica_groups=mesh['dom'=24,'grp'=32] {'dom'}, dimensions={0} | all-to-all | bytes 786432 | tf_op jit(solution)/shard_map/all_to_all | solution.py:318
  137.0 0.0 copy-start.5
  137.0 0.8 share.1
  137.8 4.6 %all-to-all-start.5 = ((bf16[32,16,256]{2,1,0:T(8,128)(2,1)}), bf16[32,16,256]{2,1,0:T(8,128)(2,1)S(1)}, u32[]{:S(2)}, u32[]{:S(2)}) async-start(bf16[32,16,256]{2,1,0:T(8,128)(2,1)} %share.1), calls=%async_computation.5 | async-start | bytes 524288 | tf_op jit(solution)/shard_map/all_to_all | solution.py:318
  142.4 0.0 copy-done.3
  142.4 4.0 %master_back.1 = (f32[1024,256]{1,0:T(8,128)}, bf16[384,256]{1,0:T(8,128)(2,1)}) custom-call(f32[1024,256]{1,0:T(8,128)} %get-tuple-element.35.refs_0_, bf16[1408,1024]{1,0:T(8,128)(2,1)} %copy-done, bf16[24,32,256]{2,1,0:T(8,128)(2,1)} %copy-done.3), custom_call_target="tpu_custom_call" | custom-call | flops 201326592 | bytes 5570560 | tf_op jit(solution)/shard_map/master_back/pallas_call | solution.py:150
  146.4 0.0 copy-done.5
  146.4 3.5 %grad.1 = bf16[1024,256]{1,0:T(8,128)(2,1)} custom-call(s32[16,24]{1,0:T(8,128)} %bitcast.9, f32[1024,256]{1,0:T(8,128)} %get-tuple-element.38.refs_1_, bf16[24,32,256]{2,1,0:T(8,128)(2,1)} %copy-done.5), custom_call_target="tpu_custom_call" | custom-call | flops 201326592 | bytes 1967616 | tf_op jit(solution)/shard_map/grad/pallas_call | solution.py:150
  149.9 3.6 %all-to-all-done.5.refs_0_ = bf16[32,16,256]{2,1,0:T(8,128)(2,1)S(1)} async-done(((bf16[32,16,256]{2,1,0:T(8,128)(2,1)}), bf16[32,16,256]{2,1,0:T(8,128)(2,1)S(1)}, u32[]{:S(2)}, u32[]{:S(2)}) %all-to-all-start.5) | async-done | bytes 262176 | tf_op jit(solution)/shard_map/all_to_all | solution.py:318
  153.5 0.8 widen.1
Async XLA Ops:
  0.6 43.8 %copy-start.14 = (f32[1024]{0:T(1024)S(1)}, f32[1024]{0:T(1024)}, u32[]{:S(2)}) copy-start(f32[1024]{0:T(1024)} %param.15) | copy-start | bytes 12292
  3.6 36.1 %all-to-all-start = ((bf16[24,32,256]{2,1,0:T(8,128)(2,1)}), bf16[24,32,256]{2,1,0:T(8,128)(2,1)S(1)}, u32[]{:S(2)}, u32[]{:S(2)}) async-start(bf16[24,32,256]{2,1,0:T(8,128)(2,1)} %pick_h.1), calls=%async_computation | async-start | bytes 786432 | tf_op jit(solution)/shard_map/all_to_all | solution.py:318
  19.0 1.0 copy-start.1
  20.0 1.2 copy-start.8
  21.2 1.0 copy-start.9
  22.2 0.7 copy-start.10
  22.9 0.7 copy-start.11
  23.6 0.7 copy-start.12
  27.7 1.6 %copy-start = (bf16[1408,1024]{1,0:T(8,128)(2,1)}, bf16[1408,1024]{1,0:T(8,128)(2,1)S(1)}, u32[]{:S(2)}) copy-start(bf16[1408,1024]{1,0:T(8,128)(2,1)S(1)} %get-tuple-element.34.refs_3_.refs_1_) | copy-start | bytes 8650756
  29.2 1.0 copy-start.2
  30.3 1.0 copy-start.7
  39.7 5.8 %copy-start.4 = (bf16[24,32,256]{2,1,0:T(8,128)(2,1)}, bf16[24,32,256]{2,1,0:T(8,128)(2,1)S(1)}, u32[]{:S(2)}) copy-start(bf16[24,32,256]{2,1,0:T(8,128)(2,1)S(1)} %all-to-all-done.refs_2_) | copy-start | bytes 1179652
  40.6 18.5 %all-to-all-start.1 = ((bf16[24,16,256]{2,1,0:T(8,128)(2,1)}), bf16[24,16,256]{2,1,0:T(8,128)(2,1)S(1)}, u32[]{:S(2)}, u32[]{:S(2)}) async-start(bf16[24,16,256]{2,1,0:T(8,128)(2,1)} %mirror_part.1), calls=%async_computation.1 | async-start | bytes 393216 | tf_op jit(solution)/shard_map/all_to_all | solution.py:318
  59.1 0.7 copy-start.13
  65.8 24.6 %all-to-all-start.2 = ((bf16[24,32,256]{2,1,0:T(8,128)(2,1)}), bf16[24,32,256]{2,1,0:T(8,128)(2,1)S(1)}, u32[]{:S(2)}, u32[]{:S(2)}) async-start(bf16[24,32,256]{2,1,0:T(8,128)(2,1)} %get-tuple-element.36), calls=%async_computation.2 | async-start | bytes 786432 | tf_op jit(solution)/shard_map/all_to_all | solution.py:318
  76.6 24.0 %copy-start.6 = (f32[384,256]{1,0:T(8,128)S(1)}, f32[384,256]{1,0:T(8,128)}, u32[]{:S(2)}) copy-start(f32[384,256]{1,0:T(8,128)} %get-tuple-element.39.refs_0_.refs_3_) | copy-start | bytes 1179652
  90.4 52.0 %copy-start.3 = (bf16[24,32,256]{2,1,0:T(8,128)(2,1)}, bf16[24,32,256]{2,1,0:T(8,128)(2,1)S(1)}, u32[]{:S(2)}) copy-start(bf16[24,32,256]{2,1,0:T(8,128)(2,1)S(1)} %all-to-all-done.2.refs_2_) | copy-start | bytes 1179652
  90.4 21.3 %all-to-all-start.3 = ((bf16[32,16,256]{2,1,0:T(8,128)(2,1)}), bf16[32,16,256]{2,1,0:T(8,128)(2,1)S(1)}, u32[]{:S(2)}, u32[]{:S(2)}) async-start(bf16[32,16,256]{2,1,0:T(8,128)(2,1)} %weights.1), calls=%async_computation.3 | async-start | bytes 524288 | tf_op jit(solution)/shard_map/all_to_all | solution.py:318
  137.0 9.4 %copy-start.5 = (bf16[24,32,256]{2,1,0:T(8,128)(2,1)}, bf16[24,32,256]{2,1,0:T(8,128)(2,1)S(1)}, u32[]{:S(2)}) copy-start(bf16[24,32,256]{2,1,0:T(8,128)(2,1)S(1)} %all_to_all.30.refs_2_.refs_0_) | copy-start | bytes 1179652
  137.8 15.7 %all-to-all-start.5 = ((bf16[32,16,256]{2,1,0:T(8,128)(2,1)}), bf16[32,16,256]{2,1,0:T(8,128)(2,1)S(1)}, u32[]{:S(2)}, u32[]{:S(2)}) async-start(bf16[32,16,256]{2,1,0:T(8,128)(2,1)} %share.1), calls=%async_computation.5 | async-start | bytes 524288 | tf_op jit(solution)/shard_map/all_to_all | solution.py:318

commit v2 on v0

--- a/solution.py
+++ b/solution.py
@@ -268,28 +268,40 @@
 
 
 def pack_kernel(rows, got, o):
-    o[:, :TILE, :] = rows[...]
+    half = o.shape[2]
     total = jnp.sum(got[...].astype(F32), axis=0).astype(BF16)
-    o[:, TILE:, :] = jnp.broadcast_to(total[None], (o.shape[0],) + total.shape)
+    for side in range(2):
+        columns = slice(side * half, (side + 1) * half)
+        o[:, side * TILE : (side + 1) * TILE, :] = rows[:, :, columns]
+    for peer in range(o.shape[0]):
+        side = peer % 2
+        o[peer, 2 * TILE :, :] = total[:, side * half : (side + 1) * half]
 
 
 def share_kernel(got, o):
-    total = jnp.sum(got[:, TILE:, :].astype(F32), axis=0).astype(BF16)
+    total = jnp.sum(got[:, 2 * TILE :, :].astype(F32), axis=0).astype(BF16)
     o[...] = jnp.broadcast_to(total[None], o.shape)
 
 
 def grad_kernel(send, back, got, o):
     spread = scatter_matrix(index_row(send[...]), o.shape[0])
-    o[...] = (back[...] + dot(spread, get_pieces(got, 0))).astype(BF16)
+    sides = [got[:, k * TILE : (k + 1) * TILE, :].reshape(got.shape[0] * TILE, got.shape[2]) for k in range(2)]
+    o[...] = (back[...] + dot(spread, jnp.concatenate(sides, axis=1))).astype(BF16)
     o.send()
 
 
-def widen_kernel(got, w_self, w_neigh):
-    half = got.shape[0] // 2
-    w_self[...] = get_pieces(got.at[:half], 0).astype(F32)
-    w_self.send()
-    w_neigh[...] = get_pieces(got.at[half:], 0).astype(F32)
-    w_neigh.send()
+def widen_kernel(core, mine, other, w_self, w_neigh):
+    half = mine.shape[2]
+    rows = mine.shape[0] * mine.shape[1]
+    ours = mine[...].reshape(rows, half).astype(F32)
+    theirs = other[...].reshape(rows, half).astype(F32)
+    first = core[0, 0] == 0
+    left = jnp.where(first, ours, theirs)
+    right = jnp.where(first, theirs, ours)
+    for into, at in ((w_self, slice(0, rows // 2)), (w_neigh, slice(rows // 2, rows))):
+        into[:, :half] = left[at, :]
+        into[:, half:] = right[at, :]
+        into.send()
 
 
 def on_device(
@@ -380,7 +392,10 @@
         "mirror_back",
         LITTLE,
     )
-    packed = call(pack_kernel, parcel(2), (mirror_back, got_terms), "vvv", 0, "pack", LITTLE)
+    half = width // 2
+    packed = call(
+        pack_kernel, sds((peers, 3 * TILE, half), BF16), (mirror_back, got_terms), "vvv", 0, "pack", LITTLE
+    )
     got_back = exchange(packed, dom)
     back, mirror_out = call(
         master_back_kernel,
@@ -390,13 +405,15 @@
         mm * rows * mirrors,
         "master_back",
     )
-    shared = call(share_kernel, parcel(1, groups), (got_back,), "vv", 0, "share", LITTLE)
+    shared = call(share_kernel, sds((groups, TILE, half), BF16), (got_back,), "vv", 0, "share", LITTLE)
     totals = exchange(shared, grp)
     grad_h = call(
         grad_kernel, wide(rows, BF16), (send, back, got_back), "vfv" + "f", mm * rows * mirrors, "grad"
     )
+    other = lax.ppermute(totals, dom, [(k, k ^ 1) for k in range(peers)])
+    core = (lax.axis_index(dom) % 2).astype(jnp.int32).reshape(1, 1)
     grad_wself, grad_wneigh = call(
-        widen_kernel, (wide(width),) * 2, (totals,), "vff", 0, "widen", LITTLE
+        widen_kernel, (wide(width),) * 2, (core, totals, other), "svvff", 0, "widen", LITTLE
     )
     return (out, mirror_out, grad_h, grad_wself, grad_wneigh)
 

time: 155 us -> 161 us (1.039)
  the two profiles are of different devices: /device:TPU:8 before, /device:TPU:1 now
where the time goes in v2:
time: 161 us; the launch traced here: 160 us
  starting transfers between devices  42.8 us (27%)
  blocking collectives  37.9 us (24%)
  Pallas kernels  37.2 us (23%)
  waiting for transfers between devices  30.6 us (19%)
  local copies, waits for them, and re-layouts  10.5 us (7%)
    all_to_all x2, blocking collectives, exchange(): return lax.all_to_all(values, axis, split_axis=0, concat_axis=0, tiled=True)  37.9 us
    all_to_all x4, starting transfers between devices, exchange(): return lax.all_to_all(values, axis, split_axis=0, concat_axis=0, tiled=True)  37.3 us
    pallas_call x13, Pallas kernels, call(): pl.pallas_call(kernel, out_shape=out, in_specs=spaces[:len(args)], out_sp...  37.2 us
    all_to_all x4, waiting for transfers between devices, exchange(): return lax.all_to_all(values, axis, split_axis=0, concat_axis=0, tiled=True)  30.6 us
    unnamed x30, local copies, waits for them, and re-layouts  9.51 us
    ppermute x1, starting transfers between devices, on_device(): other = lax.ppermute(totals, dom, [(k, k ^ 1) for k in range(peers)])  5.49 us
  transfers between devices with their start and end apart: 5, of which 4 were waited for; matrix products, arithmetic and copies ran while one was open for 1% of the time, Pallas kernels for 17%

profile of v2, /device:TPU:1, one launch (start us, length us, event | category | flops | bytes accessed | tf_op | source)
XLA Modules:
  0.0 160.0 jit_solution(898345769316875228)
XLA Ops:
  0.6 0.0 copy-start.14
  0.6 2.9 %pick_h.1 = bf16[24,32,256]{2,1,0:T(8,128)(2,1)} custom-call(s32[16,24]{1,0:T(8,128)} %bitcast.7, bf16[1024,256]{1,0:T(8,128)(2,1)} %refs_0_.3, bf16[384,256]{1,0:T(8,128)(2,1)} %refs_2_.1), custom_call_target="tpu_custom_call" | custom-call | flops 201326592 | bytes 1115648 | tf_op jit(solution)/shard_map/pick_h/pallas_call | solution.py:150
  3.6 16.7 %all-to-all-start = ((bf16[24,32,256]{2,1,0:T(8,128)(2,1)}), bf16[24,32,256]{2,1,0:T(8,128)(2,1)S(1)}, u32[]{:S(2)}, u32[]{:S(2)}) async-start(bf16[24,32,256]{2,1,0:T(8,128)(2,1)} %pick_h.1), calls=%async_computation | async-start | bytes 786432 | tf_op jit(solution)/shard_map/all_to_all | solution.py:330
  20.3 0.0 copy-start.1
  20.3 1.0 copy-done.1
  21.3 0.0 copy-start.8
  21.3 1.2 copy-done.8
  22.5 0.0 copy-start.9
  22.5 1.0 copy-done.9
  23.5 0.0 copy-start.10
  23.5 0.7 copy-done.10
  24.2 0.0 copy-start.11
  24.2 0.7 copy-done.11
  24.9 0.0 copy-start.12
  24.9 0.7 copy-done.12
  25.5 3.5 %adjacency.1 = (bf16[1408,1024]{1,0:T(8,128)(2,1)S(1)}, bf16[1408,384]{1,0:T(8,128)(2,1)S(1)}, f32[1024,256]{1,0:T(8,128)S(1)}, f32[384,256]{1,0:T(8,128)S(1)}, bf16[384,384]{1,0:T(8,128)(2,1)S(1)}) custom-call(s32[1,2]{1,0:T(1,128)S(1)} %copy-done.12, s32[2,26]{1,0:T(2,128)S(1)} %bitcast.5, s32[2,15]{1,0:T(2,128)S(1)} %bitcast.6, ...), custom_call_target="tpu_custom_call" | custom-call | flops 738197504 | bytes 7569744 | tf_op jit(solution)/shard_map/adjacency/pallas_call | solution.py:150
  29.0 0.0 copy-start
  29.0 1.5 copy-done
  30.6 0.0 copy-start.2
  30.6 1.0 copy-done.2
  31.6 0.0 copy-start.7
  31.6 1.0 copy-done.7
  32.6 5.9 %all-to-all-done.refs_2_ = bf16[24,32,256]{2,1,0:T(8,128)(2,1)S(1)} async-done(((bf16[24,32,256]{2,1,0:T(8,128)(2,1)}), bf16[24,32,256]{2,1,0:T(8,128)(2,1)S(1)}, u32[]{:S(2)}, u32[]{:S(2)}) %all-to-all-start) | async-done | bytes 393248 | tf_op jit(solution)/shard_map/all_to_all | solution.py:330
  38.5 0.0 copy-start.4
  38.5 0.9 mirror_part.1
  39.5 6.2 %all-to-all-start.1 = ((bf16[24,16,256]{2,1,0:T(8,128)(2,1)}), bf16[24,16,256]{2,1,0:T(8,128)(2,1)S(1)}, u32[]{:S(2)}, u32[]{:S(2)}) async-start(bf16[24,16,256]{2,1,0:T(8,128)(2,1)} %mirror_part.1), calls=%async_computation.1 | async-start | bytes 393216 | tf_op jit(solution)/shard_map/all_to_all | solution.py:330
  45.7 0.0 copy-done.14
  45.7 1.0 copy.17.refs_1_
  46.7 0.0 copy-done.4
  46.7 5.7 %master_part.1 = (f32[1024,256]{1,0:T(8,128)}, f32[1024,256]{1,0:T(8,128)}, f32[1024,256]{1,0:T(8,128)}) custom-call(f32[1024,256]{1,0:T(8,128)} %copy-done.7, bf16[1408,384]{1,0:T(8,128)(2,1)} %copy-done.2, bf16[24,32,256]{2,1,0:T(8,128)(2,1)} %copy-done.4, bf16[1024,256]{1,0:T(8,128)(2,1)} %refs_0_.3, bf16[256,256]{1,0:T(8,128)(2,1)} %refs_1_.3, ...), custom_call_target="tpu_custom_call" | custom-call | flops 536870912 | bytes 6850048 | tf_op jit(solution)/shard_map/master_part/pallas_call | solution.py:150
  52.4 7.0 %all-to-all-done.1.refs_5_ = bf16[24,16,256]{2,1,0:T(8,128)(2,1)S(1)} async-done(((bf16[24,16,256]{2,1,0:T(8,128)(2,1)}), bf16[24,16,256]{2,1,0:T(8,128)(2,1)S(1)}, u32[]{:S(2)}, u32[]{:S(2)}) %all-to-all-start.1) | async-done | bytes 196640 | tf_op jit(solution)/shard_map/all_to_all | solution.py:330
  59.5 0.0 copy-start.13
  59.5 0.7 copy-done.13
  60.1 5.6 %dense.1 = (bf16[1024,256]{1,0:T(8,128)(2,1)}, bf16[1024,256]{1,0:T(8,128)(2,1)}, bf16[1024,256]{1,0:T(8,128)(2,1)}, bf16[1024,256]{1,0:T(8,128)(2,1)}, bf16[24,32,256]{2,1,0:T(8,128)(2,1)}) custom-call(s32[16,24]{1,0:T(8,128)} %bitcast.9, f32[1024,1]{1,0:T(8,128)} %copy.17.refs_1_, f32[1024,256]{1,0:T(8,128)} %get-tuple-element.26.refs_2_, ...), custom_call_target="tpu_custom_call" | custom-call | flops 671088640 | bytes 5969408 | tf_op jit(solution)/shard_map/dense/pallas_call | solution.py:150
  65.8 4.7 %all-to-all-start.2 = ((bf16[24,32,256]{2,1,0:T(8,128)(2,1)}), bf16[24,32,256]{2,1,0:T(8,128)(2,1)S(1)}, u32[]{:S(2)}, u32[]{:S(2)}) async-start(bf16[24,32,256]{2,1,0:T(8,128)(2,1)} %get-tuple-element.36), calls=%async_computation.2 | async-start | bytes 786432 | tf_op jit(solution)/shard_map/all_to_all | solution.py:330
  70.5 6.8 %back.1 = (f32[1024,256]{1,0:T(8,128)}, f32[384,256]{1,0:T(8,128)}) custom-call(bf16[1024,256]{1,0:T(8,128)(2,1)} %get-tuple-element.32.refs_0_.refs_2_, bf16[256,256]{1,0:T(8,128)(2,1)} %refs_1_.3, bf16[1024,256]{1,0:T(8,128)(2,1)} %get-tuple-element.33.refs_2_, bf16[1408,1024]{1,0:T(8,128)(2,1)} %copy-done, bf16[1408,384]{1,0:T(8,128)(2,1)} %copy-done.2), custom_call_target="tpu_custom_call" | custom-call | flops 872415232 | bytes 6586368 | tf_op jit(solution)/shard_map/back/pallas_call | solution.py:150
  77.4 0.0 copy-start.6
  77.4 3.0 %weights.1 = bf16[32,16,256]{2,1,0:T(8,128)(2,1)} custom-call(bf16[1024,256]{1,0:T(8,128)(2,1)} %refs_0_.3, bf16[1024,256]{1,0:T(8,128)(2,1)} %get-tuple-element.40.refs_1_, bf16[1024,256]{1,0:T(8,128)(2,1)} %get-tuple-element.32.refs_0_.refs_2_, f32[384,256]{1,0:T(8,128)} %get-tuple-element.39.refs_0_.refs_3_), custom_call_target="tpu_custom_call" | custom-call | flops 268435456 | bytes 2228224 | tf_op jit(solution)/shard_map/weights/pallas_call | solution.py:150
  80.4 8.3 %all-to-all-done.2.refs_2_ = bf16[24,32,256]{2,1,0:T(8,128)(2,1)S(1)} async-done(((bf16[24,32,256]{2,1,0:T(8,128)(2,1)}), bf16[24,32,256]{2,1,0:T(8,128)(2,1)S(1)}, u32[]{:S(2)}, u32[]{:S(2)}) %all-to-all-start.2) | async-done | bytes 393248 | tf_op jit(solution)/shard_map/all_to_all | solution.py:330
  88.7 0.0 copy-start.3
  88.7 9.7 %all-to-all-start.3 = ((bf16[32,16,256]{2,1,0:T(8,128)(2,1)}), bf16[32,16,256]{2,1,0:T(8,128)(2,1)S(1)}, u32[]{:S(2)}, u32[]{:S(2)}) async-start(bf16[32,16,256]{2,1,0:T(8,128)(2,1)} %weights.1), calls=%async_computation.3 | async-start | bytes 524288 | tf_op jit(solution)/shard_map/all_to_all | solution.py:330
  98.4 0.0 copy-done.6
  98.4 0.3 mirror_back.1.refs_0_
  98.7 9.4 %all-to-all-done.3.refs_1_ = bf16[32,16,256]{2,1,0:T(8,128)(2,1)S(1)} async-done(((bf16[32,16,256]{2,1,0:T(8,128)(2,1)}), bf16[32,16,256]{2,1,0:T(8,128)(2,1)S(1)}, u32[]{:S(2)}, u32[]{:S(2)}) %all-to-all-start.3) | async-done | bytes 262176 | tf_op jit(solution)/shard_map/all_to_all | solution.py:330
  108.1 0.1 pack.1
  108.2 24.8 %all_to_all.30.refs_2_.refs_0_ = bf16[24,48,128]{2,1,0:T(8,128)(2,1)S(1)} all-to-all(bf16[24,48,128]{2,1,0:T(8,128)(2,1)S(1)} %pack.1), channel_id=1, replica_groups=mesh['dom'=24,'grp'=32] {'dom'}, dimensions={0} | all-to-all | bytes 589824 | tf_op jit(solution)/shard_map/all_to_all | solution.py:330
  133.0 0.0 copy-start.5
  133.1 13.1 %all_to_all.31.refs_1_ = bf16[32,16,128]{2,1,0:T(8,128)(2,1)S(1)} all-to-all(bf16[32,16,128]{2,1,0:T(8,128)(2,1)S(1)} %share.1), channel_id=1, replica_groups=mesh['dom'=24,'grp'=32] {'grp'}, dimensions={0} | all-to-all | bytes 262144 | tf_op jit(solution)/shard_map/all_to_all | solution.py:330
  146.2 5.5 %collective-permute-start = (bf16[32,16,128]{2,1,0:T(8,128)(2,1)S(1)}, bf16[32,16,128]{2,1,0:T(8,128)(2,1)S(1)}, u32[]{:S(2)}, u32[]{:S(2)}) collective-permute-start(bf16[32,16,128]{2,1,0:T(8,128)(2,1)S(1)} %all_to_all.31.refs_1_), channel_id=1, source_target_pairs={{0,32},{32,0},{64,96},{96,64},{128,160},{160,128},{192,224},{224,1... | collective-permute-start | bytes 393224 | tf_op jit(solution)/shard_map/ppermute | solution.py:413
  151.7 0.0 copy-done.3
  151.7 4.0 %master_back.1 = (f32[1024,256]{1,0:T(8,128)}, bf16[384,256]{1,0:T(8,128)(2,1)}) custom-call(f32[1024,256]{1,0:T(8,128)} %get-tuple-element.35.refs_0_, bf16[1408,1024]{1,0:T(8,128)(2,1)} %copy-done, bf16[24,32,256]{2,1,0:T(8,128)(2,1)} %copy-done.3), custom_call_target="tpu_custom_call" | custom-call | flops 201326592 | bytes 5570560 | tf_op jit(solution)/shard_map/master_back/pallas_call | solution.py:150
  155.7 0.0 copy-done.5
  155.7 3.5 %grad.1 = bf16[1024,256]{1,0:T(8,128)(2,1)} custom-call(s32[16,24]{1,0:T(8,128)} %bitcast.10, f32[1024,256]{1,0:T(8,128)} %get-tuple-element.38.refs_1_, bf16[24,48,128]{2,1,0:T(8,128)(2,1)} %copy-done.5), custom_call_target="tpu_custom_call" | custom-call | flops 201326592 | bytes 1869312 | tf_op jit(solution)/shard_map/grad/pallas_call | solution.py:150
  159.1 0.0 collective-permute-done.refs_2_
  159.1 0.8 widen.1
  (1 shorter events, 0.0 us)
Async XLA Ops:
  0.6 45.0 %copy-start.14 = (f32[1024]{0:T(1024)S(1)}, f32[1024]{0:T(1024)}, u32[]{:S(2)}) copy-start(f32[1024]{0:T(1024)} %param.15) | copy-start | bytes 12292
  3.6 34.9 %all-to-all-start = ((bf16[24,32,256]{2,1,0:T(8,128)(2,1)}), bf16[24,32,256]{2,1,0:T(8,128)(2,1)S(1)}, u32[]{:S(2)}, u32[]{:S(2)}) async-start(bf16[24,32,256]{2,1,0:T(8,128)(2,1)} %pick_h.1), calls=%async_computation | async-start | bytes 786432 | tf_op jit(solution)/shard_map/all_to_all | solution.py:330
  20.3 1.0 copy-start.1
  21.3 1.2 copy-start.8
  22.5 1.0 copy-start.9
  23.5 0.7 copy-start.10
  24.2 0.7 copy-start.11
  24.9 0.7 copy-start.12
  29.0 1.6 copy-start
  30.6 1.0 copy-start.2
  31.6 1.0 copy-start.7
  38.5 8.2 %copy-start.4 = (bf16[24,32,256]{2,1,0:T(8,128)(2,1)}, bf16[24,32,256]{2,1,0:T(8,128)(2,1)S(1)}, u32[]{:S(2)}) copy-start(bf16[24,32,256]{2,1,0:T(8,128)(2,1)S(1)} %all-to-all-done.refs_2_) | copy-start | bytes 1179652
  39.5 20.0 %all-to-all-start.1 = ((bf16[24,16,256]{2,1,0:T(8,128)(2,1)}), bf16[24,16,256]{2,1,0:T(8,128)(2,1)S(1)}, u32[]{:S(2)}, u32[]{:S(2)}) async-start(bf16[24,16,256]{2,1,0:T(8,128)(2,1)} %mirror_part.1), calls=%async_computation.1 | async-start | bytes 393216 | tf_op jit(solution)/shard_map/all_to_all | solution.py:330
  59.5 0.7 copy-start.13
  65.8 23.0 %all-to-all-start.2 = ((bf16[24,32,256]{2,1,0:T(8,128)(2,1)}), bf16[24,32,256]{2,1,0:T(8,128)(2,1)S(1)}, u32[]{:S(2)}, u32[]{:S(2)}) async-start(bf16[24,32,256]{2,1,0:T(8,128)(2,1)} %get-tuple-element.36), calls=%async_computation.2 | async-start | bytes 786432 | tf_op jit(solution)/shard_map/all_to_all | solution.py:330
  77.4 21.0 %copy-start.6 = (f32[384,256]{1,0:T(8,128)S(1)}, f32[384,256]{1,0:T(8,128)}, u32[]{:S(2)}) copy-start(f32[384,256]{1,0:T(8,128)} %get-tuple-element.39.refs_0_.refs_3_) | copy-start | bytes 1179652
  88.7 63.0 %copy-start.3 = (bf16[24,32,256]{2,1,0:T(8,128)(2,1)}, bf16[24,32,256]{2,1,0:T(8,128)(2,1)S(1)}, u32[]{:S(2)}) copy-start(bf16[24,32,256]{2,1,0:T(8,128)(2,1)S(1)} %all-to-all-done.2.refs_2_) | copy-start | bytes 1179652
  88.7 19.4 %all-to-all-start.3 = ((bf16[32,16,256]{2,1,0:T(8,128)(2,1)}), bf16[32,16,256]{2,1,0:T(8,128)(2,1)S(1)}, u32[]{:S(2)}, u32[]{:S(2)}) async-start(bf16[32,16,256]{2,1,0:T(8,128)(2,1)} %weights.1), calls=%async_computation.3 | async-start | bytes 524288 | tf_op jit(solution)/shard_map/all_to_all | solution.py:330
  133.0 22.7 %copy-start.5 = (bf16[24,48,128]{2,1,0:T(8,128)(2,1)}, bf16[24,48,128]{2,1,0:T(8,128)(2,1)S(1)}, u32[]{:S(2)}) copy-start(bf16[24,48,128]{2,1,0:T(8,128)(2,1)S(1)} %all_to_all.30.refs_2_.refs_0_) | copy-start | bytes 884740
  146.2 13.0 %collective-permute-start = (bf16[32,16,128]{2,1,0:T(8,128)(2,1)S(1)}, bf16[32,16,128]{2,1,0:T(8,128)(2,1)S(1)}, u32[]{:S(2)}, u32[]{:S(2)}) collective-permute-start(bf16[32,16,128]{2,1,0:T(8,128)(2,1)S(1)} %all_to_all.31.refs_1_), channel_id=1, source_target_pairs={{0,32},{32,0},{64,96},{96,64},{128,160},{160,128},{192,224},{224,1... | collective-permute-start | bytes 393224 | tf_op jit(solution)/shard_map/ppermute | solution.py:413
